TPU v7x, 32 devices: a whole 2x2x4 slice. The times are simulated.
32 devices in a mesh: row: 4 (over y, x), col: 8 (over z, core).
Axes of the slice: x: 2, y: 2, z: 4, core: 2. Of those that a mesh axis runs over, the one named last changes fastest.
Arguments:
- qkv: bfloat16 [1536, 3, 4096], P('row', None, 'col'), may hold values from -22 to 22
- out_weight: bfloat16 [4096, 8192], P(None, 'col'), may hold values from -0.09375 to 0.09375
- cotangent: bfloat16 [1536, 8192], P('row', 'col'), may hold values from -6 to 6
- scene_lengths: int32 [32], P('row'), may hold values from 8 to 328, as said below
- bucket_ids: int32 [32], P('row'), may hold values from 0 to 7
- sensor_ids: int32 [32], P('row'), may hold values from 0 to 7
- gsd_ids: int32 [32], P('row'), may hold values from 0 to 15
- step_ids: int32 [32], P('row'), may hold values from 0 to 999
- step_table: bfloat16 [1000, 8192], P(None, 'col'), may hold values from -3 to 3
- gsd_table: bfloat16 [16, 8192], P(None, 'col'), may hold values from -3 to 3
- sensor_table: bfloat16 [8, 8192], P(None, 'col'), may hold values from -3 to 3
- bucket_table: bfloat16 [8, 8192], P(None, 'col'), may hold values from -3 to 3
Outputs:
- mixed: bfloat16 [1536, 8192], P('row', 'col')
- grad_qkv: bfloat16 [1536, 3, 4096], P('row', None, 'col')
- grad_weight: bfloat16 [4096, 8192], P(None, 'col')
Inputs may be any that keep to these rules, and one draw needn't show every extreme that they name: `scene_lengths`: each block of 384 tokens holds 8 scenes whose lengths are positive multiples of 8 and sum to 384.
All inputs are finite; a program needn't handle non-finite values.
Results may differ from a plain program's by a relative error of at most 0.03.
Values may be sent and summed in bfloat16 or wider, within the bound.
A program may use at most 128 MiB of HBM per device.

v0:
```python
import jax
import jax.numpy as jnp
from jax import lax
from jax.sharding import PartitionSpec as P

HEAD = 128


def scene_of(lengths, count):
    ends = jnp.cumsum(lengths)
    places = jnp.arange(count)
    return jnp.sum((places[:, None] >= ends[None, :]).astype(jnp.int32), axis=1)


def lookup(ids, table):
    picks = (ids[:, None] == jnp.arange(table.shape[0])[None, :]).astype(table.dtype)
    return jnp.dot(picks, table, preferred_element_type=jnp.float32)


def attend(queries, keys, values, same):
    factor = HEAD ** (-0.5)
    scores = jnp.einsum("the,she->hts", queries, keys, preferred_element_type=jnp.float32) * factor
    scores = jnp.where(same[None], scores, -1e30)
    top = jnp.max(scores, axis=-1, keepdims=True)
    weights = jnp.exp(scores - top)
    probs = weights / jnp.sum(weights, axis=-1, keepdims=True)
    rounded = probs.astype(jnp.bfloat16)
    output = jnp.einsum("hts,she->the", rounded, values, preferred_element_type=jnp.float32).astype(
        jnp.bfloat16
    )
    return (probs, rounded, output)


def attend_back(queries, keys, values, probs, rounded, upstream):
    factor = HEAD ** (-0.5)
    grad_values = jnp.einsum(
        "hts,the->she", rounded, upstream, preferred_element_type=jnp.float32
    ).astype(jnp.bfloat16)
    grad_probs = jnp.einsum("the,she->hts", upstream, values, preferred_element_type=jnp.float32)
    inner = jnp.sum(probs * grad_probs, axis=-1, keepdims=True)
    grad_scores = (probs * (grad_probs - inner)).astype(jnp.bfloat16)
    grad_queries = (
        jnp.einsum("hts,she->the", grad_scores, keys, preferred_element_type=jnp.float32) * factor
    ).astype(jnp.bfloat16)
    grad_keys = (
        jnp.einsum("hts,the->she", grad_scores, queries, preferred_element_type=jnp.float32)
        * factor
    ).astype(jnp.bfloat16)
    stacked = jnp.stack([grad_queries, grad_keys, grad_values], axis=1)
    return stacked.reshape(stacked.shape[0], 3, stacked.shape[2] * stacked.shape[3])


def on_device(
    qkv,
    out_weight,
    cotangent,
    scene_lengths,
    bucket_ids,
    sensor_ids,
    gsd_ids,
    step_ids,
    step_table,
    gsd_table,
    sensor_table,
    bucket_table,
):
    tok_rows = qkv.shape[0]
    local_width = qkv.shape[2]
    heads_here = local_width // HEAD
    gate_scene = lookup(step_ids, step_table) + lookup(gsd_ids, gsd_table)
    gate_scene = gate_scene + lookup(sensor_ids, sensor_table) + lookup(bucket_ids, bucket_table)
    segments = scene_of(scene_lengths, tok_rows)
    member = (segments[:, None] == jnp.arange(scene_lengths.shape[0])[None, :]).astype(jnp.float32)
    gate = jnp.dot(
        member, gate_scene, precision=lax.Precision.HIGHEST, preferred_element_type=jnp.float32
    )
    same = segments[:, None] == segments[None, :]
    block = qkv.reshape(tok_rows, 3, heads_here, HEAD)
    queries = block[:, 0]
    keys = block[:, 1]
    values = block[:, 2]
    probs, rounded, attended = attend(queries, keys, values, same)
    attended = attended.reshape(tok_rows, local_width)
    rows = out_weight
    projected = jnp.dot(
        lax.all_gather(attended, "col", axis=1, tiled=True),
        rows,
        preferred_element_type=jnp.float32,
    )
    mixed = (gate * projected).astype(jnp.bfloat16)
    gated = (gate * cotangent.astype(jnp.float32)).astype(jnp.bfloat16)
    rows = out_weight
    summed = lax.psum_scatter(
        lax.dot_general(
            rows, gated, (((1,), (1,)), ((), ())), preferred_element_type=jnp.float32
        ).astype(jnp.bfloat16),
        "col",
        scatter_dimension=0,
        tiled=True,
    )
    upstream = summed.T.reshape(tok_rows, heads_here, HEAD)
    grad_qkv = attend_back(queries, keys, values, probs, rounded, upstream)
    partial_sum = lax.dot_general(
        lax.all_gather(attended, "col", axis=1, tiled=True),
        gated,
        (((0,), (0,)), ((), ())),
        preferred_element_type=jnp.float32,
    )
    total = lax.psum(partial_sum.astype(jnp.bfloat16), "row")
    return (mixed, grad_qkv, total)


def solution(mesh):
    return jax.shard_map(
        on_device,
        mesh=mesh,
        in_specs=(
            P("row", None, "col"),
            P(None, "col"),
            P("row", "col"),
            P("row"),
            P("row"),
            P("row"),
            P("row"),
            P("row"),
            P(None, "col"),
            P(None, "col"),
            P(None, "col"),
            P(None, "col"),
        ),
        out_specs=(P("row", "col"), P("row", None, "col"), P(None, "col")),
        check_vma=False,
    )
```

profile of v0, /device:TPU:0, one launch (start us, length us, event | category | flops | bytes accessed | tf_op | source)
XLA Modules:
  0.0 287.8 jit_solution(9080995188754259612)
XLA Ops:
  7.2 1.0 reduce-window.8
  8.2 0.1 convert_reduce_fusion
  8.3 0.1 broadcast_compare_fusion
  8.4 1.7 copy.42
  10.2 2.3 fusion.21
  12.5 2.9 convolution_convert_fusion.2
  15.5 0.4 fusion.14
  15.9 0.2 copy-done.4
  16.1 0.2 convolution_add_fusion.2
  16.3 0.2 convolution_add_fusion.1
  16.5 0.2 convolution_add_fusion
  16.7 0.8 fusion.12
  17.5 1.2 copy-done.1
  18.7 10.4 %fusion.1 = bf16[4096,384]{0,1:T(8,128)(2,1)} fusion(bf16[4096,1024]{1,0:T(8,128)(2,1)} %param.13, f32[384,1024]{1,0:T(8,128)S(1)} %fusion.12, bf16[384,1024]{1,0:T(8,128)(2,1)S(1)} %copy-done.11), kind=kOutput, calls=%fused_computation.3 | convolution fusion | flops 3223977984 | bytes 13893632 | tf_op jit(solution)/shard_map/dot_general | solution.py:94
  29.1 0.2 all-reduce.2.cloned.1.call-start
  29.3 27.2 %all-gather.2.cloned.1.call-done = bf16[384,4096]{0,1:T(8,128)(2,1)} async-done(((bf16[384,512]{0,1:T(8,128)(2,1)}), bf16[384,4096]{0,1:T(8,128)(2,1)}) %all-gather.2.cloned.1.call-update) | async-done | bytes 3145744 | tf_op jit(solution)/shard_map/all_gather | solution.py:86
  56.6 10.5 %convolution_convert_fusion = bf16[4096,1024]{1,0:T(8,128)(2,1)} fusion(bf16[384,4096]{0,1:T(8,128)(2,1)} %all-gather.2.cloned.1.call-done, f32[384,1024]{1,0:T(8,128)} %copy-done.1, bf16[384,1024]{1,0:T(8,128)(2,1)} %param.14), kind=kOutput, calls=%fused_computation.1 | convolution fusion | flops 3226599424 | bytes 13893632 | tf_op jit(solution)/shard_map/dot_general | solution.py:103
  67.1 9.1 %multiply_convert_fusion.2 = bf16[384,1024]{1,0:T(8,128)(2,1)} fusion(f32[384,1024]{1,0:T(8,128)} %copy-done.1, bf16[384,4096]{0,1:T(8,128)(2,1)} %all-gather.2.cloned.1.call-done, bf16[4096,1024]{1,0:T(8,128)(2,1)} %param.13), kind=kOutput, calls=%fused_computation.10 | convolution fusion | flops 3222011904 | bytes 13893632 | tf_op jit(solution)/shard_map/dot_general | solution.py:85
  76.2 22.0 %reduce-scatter.2.cloned.1.call-done = bf16[512,384]{0,1:T(8,128)(2,1)} async-done(((bf16[4096,384]{0,1:T(8,128)(2,1)}), bf16[512,384]{0,1:T(8,128)(2,1)}) %reduce-scatter.2.cloned.1.call-update) | async-done | bytes 393232 | tf_op jit(solution)/shard_map/reduce_scatter | solution.py:93
  98.1 1.9 copy.66
  100.0 3.1 %convolution_convert_fusion.3 = bf16[4,128,384]{2,1,0:T(8,128)(2,1)} fusion(bf16[384,4,128]{0,2,1:T(8,128)(2,1)} %bitcast.74, f32[4,384,384]{1,2,0:T(8,128)} %get-tuple-element.4, f32[4,384]{1,0:T(4,128)S(1)} %get-tuple-element.3), kind=kOutput, calls=%fused_computation.16 | convolution fusion | flops 152371200 | bytes 3151872 | tf_op jit(solution)/shard_map/hts,the->she/dot_general | solution.py:36
  103.1 2.0 copy.56
  105.1 2.8 multiply_reduce_fusion
  107.9 0.6 copy-done.2
  108.5 0.4 multiply_convert_fusion
  108.9 2.2 fusion.4
  111.1 2.0 copy.54
  113.0 2.3 fusion.3
  115.3 1.2 copy.55
  116.5 2.3 pad_maximum_fusion
  118.7 154.7 %all-reduce.2.cloned.1.call-done = bf16[4096,1024]{1,0:T(8,128)(2,1)} async-done(((bf16[4096,1024]{1,0:T(8,128)(2,1)}), bf16[4096,1024]{1,0:T(8,128)(2,1)}) %all-reduce.2.cloned.1.call-update) | async-done | bytes 8388624 | tf_op jit(solution)/shard_map/psum | solution.py:109
  273.5 7.8 %copy.68 = bf16[4096,1024]{1,0:T(8,128)(2,1)} copy(bf16[4096,1024]{1,0:T(8,128)(2,1)} %all-reduce.2.cloned.1.call-done) | data formatting | bytes 16777216
  (26 shorter events, 0.2 us)
Async XLA Ops:
  7.2 8.3 %copy-start = (bf16[1000,1024]{1,0:T(8,128)(2,1)S(1)}, bf16[1000,1024]{1,0:T(8,128)(2,1)}, u32[]{:S(2)}) copy-start(bf16[1000,1024]{1,0:T(8,128)(2,1)} %param.20) | copy-start | bytes 6144004
  7.2 49.4 %all-gather.2.cloned.1.call-start = ((), (), s32[]{:S(2)}) async-start(), calls=%async_computation.1 | async-start | bytes 3538944 | tf_op jit(solution)/shard_map/all_gather | solution.py:86
  10.1 95.0 %copy-start.3 = (bf16[384,3,512]{0,2,1:T(8,128)(2,1)}, bf16[384,3,512]{0,2,1:T(8,128)(2,1)S(1)}, u32[]{:S(2)}) copy-start(bf16[384,3,512]{0,2,1:T(8,128)(2,1)S(1)} %copy.42) | copy-start | bytes 3538948
  12.5 3.0 %copy-start.7 = (s32[8]{0:T(128)S(1)}, s32[8]{0:T(128)}, u32[]{:S(2)}) copy-start(s32[8]{0:T(128)} %param.19) | copy-start | bytes 100
  15.4 0.8 copy-start.4
  15.4 0.8 copy-start.8
  15.4 0.9 copy-start.5
  15.4 0.9 copy-start.9
  15.4 1.1 copy-start.6
  15.4 1.1 copy-start.10
  15.4 82.7 %reduce-scatter.2.cloned.1.call-start = ((), (), s32[]{:S(2)}) async-start(), calls=%async_computation.2 | async-start | bytes 3538944 | tf_op jit(solution)/shard_map/reduce_scatter | solution.py:93
  15.5 3.2 %copy-start.11 = (bf16[384,1024]{1,0:T(8,128)(2,1)S(1)}, bf16[384,1024]{1,0:T(8,128)(2,1)}, u32[]{:S(2)}) copy-start(bf16[384,1024]{1,0:T(8,128)(2,1)} %param.14) | copy-start | bytes 2359300
  17.5 1.2 copy-start.1
  29.1 244.4 %all-reduce.2.cloned.1.call-start = ((), (), s32[]{:S(2)}) async-start(), calls=%async_computation.3 | async-start | bytes 16777216 | tf_op jit(solution)/shard_map/psum | solution.py:109
  105.1 3.4 %copy-start.2 = (f32[4,384,384]{1,2,0:T(8,128)S(1)}, f32[4,384,384]{1,2,0:T(8,128)}, u32[]{:S(2)}) copy-start(f32[4,384,384]{1,2,0:T(8,128)} %get-tuple-element.4) | copy-start | bytes 7077892
Sparse Core Ops, SparseCore 0:
  15.5 40.9 all-gather.1
  58.9 39.2 reduce-scatter.1
  102.2 171.1 all-reduce.1
where the time goes:
time: 288 us
  waiting for transfers between devices  204 us (71%)
  matrix products  47.4 us (16%)
  local copies, waits for them, and re-layouts  18.4 us (6%)
  between operations  13.9 us (5%)
  other arithmetic  3.83 us (1%)
    psum x1, waiting for transfers between devices, on_device(): total = lax.psum(partial_sum.astype(jnp.bfloat16), 'row')  155 us
    all_gather x1, waiting for transfers between devices, on_device(): lax.all_gather(attended, 'col', axis=1, tiled=True)  27.2 us
    reduce_scatter x1, waiting for transfers between devices, on_device(): lax.psum_scatter(lax.dot_general(rows, gated, (((1,), (1,)), ((), ())), p...  22 us
    unnamed x26, local copies, waits for them, and re-layouts  11.4 us
    dot_general x1, matrix products, on_device(): lax.dot_general(lax.all_gather(attended, 'col', axis=1, tiled=True), gate...  10.5 us
    dot_general x1, matrix products, on_device(): lax.dot_general(rows, gated, (((1,), (1,)), ((), ())), preferred_element_...  10.4 us
    dot_general x1, matrix products, on_device(): jnp.dot(lax.all_gather(attended, 'col', axis=1, tiled=True), rows, prefer...  9.08 us
  transfers between devices with their start and end apart: 3, of which 3 were waited for; matrix products, arithmetic and copies ran while one was open for 18% of the time, Pallas kernels for 0%

commit v1 on v0

--- a/solution.py
+++ b/solution.py
@@ -1,6 +1,8 @@
 import jax
 import jax.numpy as jnp
 from jax import lax
+from jax.experimental import pallas as pl
+from jax.experimental.pallas import tpu as pltpu
 from jax.sharding import PartitionSpec as P
 
 HEAD = 128
@@ -110,9 +112,437 @@
     return (mixed, grad_qkv, total)
 
 
+def dot(a, b, dims):
+    return lax.dot_general(a, b, (dims, ((), ())), preferred_element_type=jnp.float32)
+
+
+def remote(src, dst, send, recv, device):
+    return pltpu.make_async_remote_copy(
+        src_ref=src,
+        dst_ref=dst,
+        send_sem=send,
+        recv_sem=recv,
+        device_id=device,
+        device_id_type=pl.DeviceIdType.MESH,
+    )
+
+
+def fused_kernel(
+    lengths,
+    qkv,
+    weight_hbm,
+    cotangent,
+    gate_scene,
+    mixed_out,
+    grad_out,
+    total_hbm,
+    weight,
+    att,
+    gat,
+    gate,
+    total_acc,
+    probs_s,
+    own,
+    pair_send,
+    pair_recv,
+    line_send,
+    line_recv,
+    upstream,
+    w_sem,
+    out_sem,
+    att_recv,
+    gat_recv,
+    pr_recv,
+    lr_recv,
+    z_sent,
+    x_sent,
+    y_sent,
+    fx_sent,
+    fy_sent,
+    p_sent,
+    g_sent,
+    ps_sent,
+    ls_sent,
+):
+    tok, width = cotangent.shape
+    local = qkv.shape[2]
+    heads = local // HEAD
+    half = tok // 2
+    nb = weight.shape[0]
+    nz = nb // 2
+    scenes = gate_scene.shape[0]
+    factor = HEAD ** (-0.5)
+    r = lax.axis_index("row")
+    col = lax.axis_index("col")
+    z = col // 2
+    k = lax.rem(col, 2)
+    xn = r + 1 - 2 * lax.rem(r, 2)
+    yn = lax.rem(r + 2, 4)
+    dn = 3 - r
+    pair = {"col": col + 1 - 2 * k}
+    to_x = {"row": xn}
+    to_y = {"row": yn}
+
+    barrier = pltpu.get_barrier_semaphore()
+    peers = [pair, to_x, to_y] + [{"col": 2 * lax.rem(z + d, nz) + k} for d in range(1, nz)]
+    for peer in peers:
+        pl.semaphore_signal(
+            barrier, inc=1, device_id=peer, device_id_type=pl.DeviceIdType.MESH
+        )
+    pl.semaphore_wait(barrier, len(peers))
+
+    def load(b):
+        return pltpu.make_async_copy(
+            weight_hbm.at[pl.ds(b * local, local)], weight.at[b], w_sem.at[b]
+        )
+
+    for b in range(nb):
+        load(b).start()
+
+    def token_rows(row, part=None):
+        if part is None:
+            return pl.ds(pl.multiple_of(row * tok, tok), tok)
+        return pl.ds(pl.multiple_of(row * tok + part * half, half), half)
+
+    place_col = lax.broadcasted_iota(jnp.int32, (tok, 1), 0)
+    place_row = lax.broadcasted_iota(jnp.int32, (1, tok), 1)
+    seg_col = jnp.zeros((tok, 1), jnp.int32)
+    seg_row = jnp.zeros((1, tok), jnp.int32)
+    end = 0
+    for s in range(scenes):
+        end = end + lengths[s]
+        seg_col = seg_col + (place_col >= end).astype(jnp.int32)
+        seg_row = seg_row + (place_row >= end).astype(jnp.int32)
+    value = jnp.broadcast_to(gate_scene[0:1, :], (tok, width))
+    for s in range(1, scenes):
+        value = jnp.where(seg_col == s, gate_scene[s : s + 1, :], value)
+    gate[...] = value
+    gat[token_rows(r), :] = (value * cotangent[...].astype(jnp.float32)).astype(jnp.bfloat16)
+
+    def gat_copy(row, part, send, device):
+        rows = gat.at[token_rows(row, part)]
+        return remote(rows, rows, g_sent.at[send], gat_recv.at[row, 0 if part is None else part], device)
+
+    gat_copy(r, None, 0, to_x).start()
+    gat_copy(r, None, 1, to_y).start()
+
+    same = seg_col == seg_row
+    mine = 2 * z + k
+    for h in range(heads):
+        lanes = slice(h * HEAD, (h + 1) * HEAD)
+        scores = dot(qkv[0, :, lanes], qkv[1, :, lanes], ((1,), (1,))) * factor
+        scores = jnp.where(same, scores, -1e30)
+        top = jnp.max(scores, axis=-1, keepdims=True)
+        weights = jnp.exp(scores - top)
+        probs = weights / jnp.sum(weights, axis=-1, keepdims=True)
+        probs_s[h] = probs
+        out = dot(probs.astype(jnp.bfloat16), qkv[2, :, lanes], ((1,), (0,)))
+        att[mine, token_rows(r), lanes] = out.astype(jnp.bfloat16)
+
+    orders = [sorted(range(nz), key=lambda o: (abs(o - p), o)) for p in range(nz)]
+
+    def origin(j):
+        picked = orders[0][j]
+        for p in range(1, nz):
+            picked = jnp.where(z == p, orders[p][j], picked)
+        return picked
+
+    origins = [origin(j) for j in range(nz)]
+
+    def block(row, b, part=None):
+        return att.at[b, token_rows(row, part)]
+
+    def att_copy(row, b, part, send, device):
+        ref = block(row, b, part)
+        return remote(ref, ref, send, att_recv.at[row, b, 0 if part is None else part], device)
+
+    def pass_on(row, o):
+        return att_copy(row, 2 * o + k, None, p_sent.at[row, o], pair)
+
+    def got(row, b, part=None):
+        att_copy(row, b, part, p_sent.at[0, 0], pair).wait_recv()
+
+    def upward(o):
+        return att_copy(r, 2 * o + k, None, z_sent.at[o, 0], {"col": lax.rem(col + 2, 2 * nz)})
+
+    def downward(o):
+        return att_copy(
+            r, 2 * o + k, None, z_sent.at[o, 1], {"col": lax.rem(col + 2 * nz - 2, 2 * nz)}
+        )
+
+    def stage_a(j):
+        o = origins[j]
+        if j > 0:
+            got(r, 2 * o + k)
+
+        @pl.when((o <= z) & (z < nz - 1))
+        def _():
+            upward(o).start()
+
+        @pl.when((o >= z) & (z > 0))
+        def _():
+            downward(o).start()
+
+        att_copy(r, 2 * o + k, None, x_sent.at[j], to_x).start()
+        att_copy(r, 2 * o + k, None, y_sent.at[j], to_y).start()
+        pass_on(r, o).start()
+
+    def stage_b(j):
+        o = origins[j]
+        b = 2 * o + k
+        got(xn, b)
+        att_copy(xn, b, 0, fy_sent.at[j], to_y).start()
+        pass_on(xn, o).start()
+        got(yn, b)
+        att_copy(yn, b, 1, fx_sent.at[j], to_x).start()
+        pass_on(yn, o).start()
+
+    def stage_c(j):
+        o = origins[j]
+        got(dn, 2 * o + k, 0)
+        got(dn, 2 * o + k, 1)
+        pass_on(dn, o).start()
+
+    def stage_m(j):
+        o = origins[j]
+        got(r, 2 * o + 1 - k)
+
+        def add(c, carry):
+            b = 2 * o + c
+            term = dot(att[b, token_rows(r), :], weight[b], ((1,), (0,)))
+            if j == 0:
+                total_acc[c] = term
+            else:
+                total_acc[c] += term
+            return carry
+
+        lax.fori_loop(0, 2, add, 0)
+
+    def out_copy(b):
+        return pltpu.make_async_copy(
+            weight.at[b], total_hbm.at[pl.ds(pl.multiple_of(b * local, local), local)], out_sem.at[b]
+        )
+
+    def stage_w(j):
+        o = origins[j]
+        for row in (xn, yn, dn):
+            got(row, 2 * o + 1 - k)
+
+        def form(c, carry):
+            b = 2 * o + c
+            weight[b] = dot(att[b], gat[...], ((0,), (0,))).astype(jnp.bfloat16)
+            out_copy(b).start()
+            return carry
+
+        lax.fori_loop(0, 2, form, 0)
+
+    stage_a(0)
+
+    for b in range(nb):
+        load(b).wait()
+
+    def pair_copy(t):
+        return remote(pair_send.at[t], pair_recv.at[t], ps_sent.at[t], pr_recv.at[t], pair)
+
+    def part_of(b):
+        return dot(gat[token_rows(r), :], weight[b], ((1,), (1,)))
+
+    def for_pair(i, carry):
+        t = lax.rem(z + 1 + i, nz)
+        pair_send[t] = part_of(2 * t + 1 - k).astype(jnp.bfloat16)
+        pair_copy(t).start()
+        return carry
+
+    lax.fori_loop(0, nz, for_pair, 0)
+
+    def for_self(i, carry):
+        t = lax.rem(z + 1 + i, nz)
+        own[t] = part_of(2 * t + k)
+        return carry
+
+    lax.fori_loop(0, nz, for_self, 0)
+
+    def line_copy(t):
+        return remote(
+            line_send.at[t], line_recv.at[z], ls_sent.at[t], lr_recv.at[z], {"col": 2 * t + k}
+        )
+
+    for d in range(1, nz):
+        t = lax.rem(z + d, nz)
+        pair_copy(t).wait_recv()
+        line_send[t] = (own[t] + pair_recv[t].astype(jnp.float32)).astype(jnp.bfloat16)
+        line_copy(t).start()
+
+    stage_a(1)
+    gat_copy(xn, None, 0, to_x).wait_recv()
+    gat_copy(xn, 0, 2, to_y).start()
+    gat_copy(yn, None, 0, to_x).wait_recv()
+    gat_copy(yn, 1, 3, to_x).start()
+    stage_b(0)
+    stage_a(2)
+    stage_m(0)
+    stage_c(0)
+    stage_b(1)
+    stage_a(3)
+    stage_m(1)
+    stage_c(1)
+
+    pair_copy(z).wait_recv()
+    summed = own[z] + pair_recv[z].astype(jnp.float32)
+    for d in range(1, nz):
+        t = lax.rem(z + d, nz)
+        remote(
+            line_send.at[t], line_recv.at[t], ls_sent.at[t], lr_recv.at[t], {"col": 2 * t + k}
+        ).wait_recv()
+        summed = summed + line_recv[t].astype(jnp.float32)
+    upstream[...] = summed.astype(jnp.bfloat16)
+    for h in range(heads):
+        lanes = slice(h * HEAD, (h + 1) * HEAD)
+        upper = upstream[:, lanes]
+        probs = probs_s[h]
+        grad_out[2, :, lanes] = dot(probs.astype(jnp.bfloat16), upper, ((0,), (0,))).astype(
+            jnp.bfloat16
+        )
+        grad_probs = dot(upper, qkv[2, :, lanes], ((1,), (1,)))
+        inner = jnp.sum(probs * grad_probs, axis=-1, keepdims=True)
+        grad_scores = (probs * (grad_probs - inner)).astype(jnp.bfloat16)
+        grad_out[0, :, lanes] = (
+            dot(grad_scores, qkv[1, :, lanes], ((1,), (0,))) * factor
+        ).astype(jnp.bfloat16)
+        grad_out[1, :, lanes] = (
+            dot(grad_scores, qkv[0, :, lanes], ((0,), (0,))) * factor
+        ).astype(jnp.bfloat16)
+
+    stage_b(2)
+    stage_m(2)
+    stage_m(3)
+    mixed_out[...] = (gate[...] * (total_acc[0] + total_acc[1])).astype(jnp.bfloat16)
+    gat_copy(dn, 0, 0, to_x).wait_recv()
+    gat_copy(dn, 1, 0, to_x).wait_recv()
+    stage_c(2)
+    stage_w(0)
+    stage_b(3)
+    stage_w(1)
+    stage_c(3)
+    stage_w(2)
+    stage_w(3)
+
+    gat_copy(r, None, 0, to_x).wait_send()
+    gat_copy(r, None, 1, to_y).wait_send()
+    gat_copy(xn, 0, 2, to_y).wait_send()
+    gat_copy(yn, 1, 3, to_x).wait_send()
+    for j in range(nz):
+        o = origins[j]
+        b = 2 * o + k
+
+        @pl.when((o <= z) & (z < nz - 1))
+        def _():
+            upward(o).wait_send()
+
+        @pl.when((o >= z) & (z > 0))
+        def _():
+            downward(o).wait_send()
+
+        att_copy(r, b, None, x_sent.at[j], to_x).wait_send()
+        att_copy(r, b, None, y_sent.at[j], to_y).wait_send()
+        att_copy(xn, b, 0, fy_sent.at[j], to_y).wait_send()
+        att_copy(yn, b, 1, fx_sent.at[j], to_x).wait_send()
+        for row in (r, xn, yn, dn):
+            pass_on(row, o).wait_send()
+        pair_copy(j).wait_send()
+        out_copy(2 * j).wait()
+        out_copy(2 * j + 1).wait()
+    for d in range(1, nz):
+        line_copy(lax.rem(z + d, nz)).wait_send()
+
+
+def fused_device(
+    qkv,
+    out_weight,
+    cotangent,
+    scene_lengths,
+    bucket_ids,
+    sensor_ids,
+    gsd_ids,
+    step_ids,
+    step_table,
+    gsd_table,
+    sensor_table,
+    bucket_table,
+):
+    rows = lax.axis_size("row")
+    cols = lax.axis_size("col")
+    nz = cols // 2
+    tok, width = cotangent.shape
+    local = qkv.shape[2]
+    gate_scene = lookup(step_ids, step_table) + lookup(gsd_ids, gsd_table)
+    gate_scene = gate_scene + lookup(sensor_ids, sensor_table) + lookup(bucket_ids, bucket_table)
+    dma = pltpu.SemaphoreType.DMA
+    bf16 = jnp.bfloat16
+    mixed, grad, total = pl.pallas_call(
+        fused_kernel,
+        out_shape=(
+            jax.ShapeDtypeStruct((tok, width), bf16),
+            jax.ShapeDtypeStruct((3, tok, local), bf16),
+            jax.ShapeDtypeStruct(out_weight.shape, bf16),
+        ),
+        in_specs=[
+            pl.BlockSpec(memory_space=pltpu.SMEM),
+            pl.BlockSpec(memory_space=pltpu.VMEM),
+            pl.BlockSpec(memory_space=pl.ANY),
+            pl.BlockSpec(memory_space=pltpu.VMEM),
+            pl.BlockSpec(memory_space=pltpu.VMEM),
+        ],
+        out_specs=(
+            pl.BlockSpec(memory_space=pltpu.VMEM),
+            pl.BlockSpec(memory_space=pltpu.VMEM),
+            pl.BlockSpec(memory_space=pl.ANY),
+        ),
+        scratch_shapes=[
+            pltpu.VMEM((cols, local, width), bf16),
+            pltpu.VMEM((cols, rows * tok, local), bf16),
+            pltpu.VMEM((rows * tok, width), bf16),
+            pltpu.VMEM((tok, width), jnp.float32),
+            pltpu.VMEM((2, tok, width), jnp.float32),
+            pltpu.VMEM((local // HEAD, tok, tok), jnp.float32),
+            pltpu.VMEM((nz, tok, local), jnp.float32),
+            pltpu.VMEM((nz, tok, local), bf16),
+            pltpu.VMEM((nz, tok, local), bf16),
+            pltpu.VMEM((nz, tok, local), bf16),
+            pltpu.VMEM((nz, tok, local), bf16),
+            pltpu.VMEM((tok, local), bf16),
+            dma((cols,)),
+            dma((cols,)),
+            dma((rows, cols, 2)),
+            dma((rows, 2)),
+            dma((nz,)),
+            dma((nz,)),
+            dma((nz, 2)),
+            dma((nz,)),
+            dma((nz,)),
+            dma((nz,)),
+            dma((nz,)),
+            dma((rows, nz)),
+            dma((4,)),
+            dma((nz,)),
+            dma((nz,)),
+        ],
+        compiler_params=pltpu.CompilerParams(
+            collective_id=0, has_side_effects=True, vmem_limit_bytes=60 * 2**20
+        ),
+        cost_estimate=pl.CostEstimate(
+            flops=2 * (rows + 2) * tok * out_weight.shape[0] * width,
+            bytes_accessed=4 * out_weight.shape[0] * width,
+            transcendentals=0,
+        ),
+    )(scene_lengths, jnp.transpose(qkv, (1, 0, 2)), out_weight, cotangent, gate_scene)
+    return (mixed, jnp.transpose(grad, (1, 0, 2)), total)
+
+
 def solution(mesh):
+    planes = mesh.shape["row"] == 4 and mesh.shape["col"] == 8
     return jax.shard_map(
-        on_device,
+        fused_device if planes else on_device,
         mesh=mesh,
         in_specs=(
             P("row", None, "col"),

time: 288 us -> 119 us (0.41)
  waiting for transfers between devices: 204 us -> 0 us
  Pallas kernels: 0 us -> 103 us
  matrix products: 47.4 us -> 2.28 us
  between operations: 13.9 us -> 0.72 us
  local copies, waits for them, and re-layouts: 18.4 us -> 12.5 us
  other arithmetic: 3.83 us -> 0 us
    psum x1 -> x0, waiting for transfers between devices: 155 us -> none  [on_device(): total = lax.psum(partial_sum.astype(jnp.bfloat16), 'row')]
    pallas_call x0 -> x1, Pallas kernels: none -> 103 us  [fused_device(): pl.pallas_call(fused_kernel, out_shape=(jax.ShapeDtypeStruct((tok, width)...]
    dot_general x9 -> x0, matrix products: 44 us -> none  [the longest x1 10.5 us: on_device(): lax.dot_general(lax.all_gather(attended, 'col', axis=1, tiled=True), gate...]
    all_gather x1 -> x0, waiting for transfers between devices: 27.2 us -> none  [on_device(): lax.all_gather(attended, 'col', axis=1, tiled=True)]
    reduce_scatter x1 -> x0, waiting for transfers between devices: 22 us -> none  [on_device(): lax.psum_scatter(lax.dot_general(rows, gated, (((1,), (1,)), ((), ())), p...]
    another operation x3 -> x0, local copies, waits for them, and re-layouts: 5.1 us -> none  [attend_back(): stacked = jnp.stack([grad_queries, grad_keys, grad_values], axis=1)]
    another operation x2 -> x0, other arithmetic: 3.22 us -> none  [the longest x1 2.26 us: attend_back(): stacked = jnp.stack([grad_queries, grad_keys, grad_values], axis=1)]
    unnamed x26 -> x19, local copies, waits for them, and re-layouts: 11.4 us -> 12.5 us
  transfers between devices with their start and end apart: 3 -> 0, of which waited for: 3 -> 0; matrix products, arithmetic and copies ran while one was open for 18% -> 0% of each run, Pallas kernels for 0% -> 0%
where the time goes in v1:
time: 119 us
  Pallas kernels  103 us (87%)
  local copies, waits for them, and re-layouts  12.5 us (11%)
  matrix products  2.28 us (2%)
    pallas_call x1, Pallas kernels, fused_device(): pl.pallas_call(fused_kernel, out_shape=(jax.ShapeDtypeStruct((tok, width)...  103 us
    unnamed x19, local copies, waits for them, and re-layouts  12.5 us

profile of v1, /device:TPU:0, one launch (start us, length us, event | category | flops | bytes accessed | tf_op | source)
XLA Modules:
  0.0 118.9 jit_solution(13524666623187803448)
XLA Ops:
  0.6 0.0 copy-start
  0.6 0.0 copy-start.4
  0.7 0.0 copy-start.3
  0.7 0.0 copy-start.2
  0.7 0.0 copy-start.5
  0.7 0.0 copy-start.6
  0.7 0.0 copy-start.7
  0.7 1.6 %copy-done = bf16[1000,1024]{1,0:T(8,128)(2,1)S(1)} copy-done((bf16[1000,1024]{1,0:T(8,128)(2,1)S(1)}, bf16[1000,1024]{1,0:T(8,128)(2,1)}, u32[]{:S(2)}) %copy-start) | copy-done | bytes 2048024
  2.3 1.1 fusion
  3.4 0.0 copy-done.2
  3.4 0.0 copy-done.5
  3.4 0.2 convolution_add_fusion.2
  3.6 0.0 copy-done.3
  3.6 0.0 copy-done.6
  3.6 0.2 convolution_add_fusion.1
  3.8 0.0 copy-done.4
  3.8 0.0 copy-done.7
  3.8 0.8 convolution_add_fusion.gate_scene
  4.6 103.3 %shard_map.139 = (bf16[384,1024]{1,0:T(8,128)(2,1)}, bf16[3,384,512]{2,1,0:T(8,128)(2,1)}, bf16[4096,1024]{1,0:T(8,128)(2,1)}) custom-call(s32[8]{0:T(128)} %lengths.1, bf16[3,384,512]{2,1,0:T(8,128)(2,1)} %bitcast.7, bf16[4096,1024]{1,0:T(8,128)(2,1)} %weight_hbm.1, bf16[384,1024]{1,0:T(8,128)(2,1)} %cotangent.1, f32[8,1024]{1,0:T(8,128)} %convolution_add_fusion.gate_scene), custom_call_target="tpu_custom_call" | custom-call | flops 19327352832 | bytes 16777216 | tf_op jit(solution)/shard_map/pallas_call | solution.py:482
  107.9 0.0 copy-start.1
  108.0 2.2 %copy.18 = bf16[384,1024]{1,0:T(8,128)(2,1)} copy(bf16[384,1024]{1,0:T(8,128)(2,1)} %get-tuple-element.12) | data formatting | bytes 1572864
  110.1 0.0 copy-done.1
  110.1 1.0 copy.19
  111.1 7.8 %copy.20 = bf16[4096,1024]{1,0:T(8,128)(2,1)} copy(bf16[4096,1024]{1,0:T(8,128)(2,1)} %get-tuple-element.14) | data formatting | bytes 16777216
Async XLA Ops:
  0.6 1.6 %copy-start = (bf16[1000,1024]{1,0:T(8,128)(2,1)S(1)}, bf16[1000,1024]{1,0:T(8,128)(2,1)}, u32[]{:S(2)}) copy-start(bf16[1000,1024]{1,0:T(8,128)(2,1)} %param.20) | copy-start | bytes 6144004
  0.6 3.1 %copy-start.4 = (bf16[8,1024]{1,0:T(8,128)(2,1)S(1)}, bf16[8,1024]{1,0:T(8,128)(2,1)}, u32[]{:S(2)}) copy-start(bf16[8,1024]{1,0:T(8,128)(2,1)} %param.23) | copy-start | bytes 49156
  0.7 2.9 %copy-start.3 = (bf16[8,1024]{1,0:T(8,128)(2,1)S(1)}, bf16[8,1024]{1,0:T(8,128)(2,1)}, u32[]{:S(2)}) copy-start(bf16[8,1024]{1,0:T(8,128)(2,1)} %param.22) | copy-start | bytes 49156
  0.7 2.7 %copy-start.2 = (bf16[16,1024]{1,0:T(8,128)(2,1)S(1)}, bf16[16,1024]{1,0:T(8,128)(2,1)}, u32[]{:S(2)}) copy-start(bf16[16,1024]{1,0:T(8,128)(2,1)} %param.21) | copy-start | bytes 98308
  0.7 2.7 %copy-start.5 = (s32[8]{0:T(128)S(1)}, s32[8]{0:T(128)}, u32[]{:S(2)}) copy-start(s32[8]{0:T(128)} %param.18) | copy-start | bytes 100
  0.7 2.9 %copy-start.6 = (s32[8]{0:T(128)S(1)}, s32[8]{0:T(128)}, u32[]{:S(2)}) copy-start(s32[8]{0:T(128)} %param.17) | copy-start | bytes 100
  0.7 3.1 %copy-start.7 = (s32[8]{0:T(128)S(1)}, s32[8]{0:T(128)}, u32[]{:S(2)}) copy-start(s32[8]{0:T(128)} %param.16) | copy-start | bytes 100
  107.9 2.2 %copy-start.1 = (bf16[3,384,512]{2,1,0:T(8,128)(2,1)S(1)}, bf16[3,384,512]{2,1,0:T(8,128)(2,1)}, u32[]{:S(2)}) copy-start(bf16[3,384,512]{2,1,0:T(8,128)(2,1)} %get-tuple-element.7) | copy-start | bytes 3538948

commit v2 on v1

--- a/solution.py
+++ b/solution.py
@@ -127,15 +127,106 @@
     )
 
 
+def origins_of(z, nz):
+    orders = [sorted(range(nz), key=lambda o: (abs(o - p), o)) for p in range(nz)]
+    origins = []
+    for j in range(nz):
+        picked = orders[0][j]
+        for p in range(1, nz):
+            picked = jnp.where(z == p, orders[p][j], picked)
+        origins.append(picked)
+    return origins
+
+
+def last_kernel(
+    mixed_in,
+    grad_in,
+    total_head,
+    att_tail,
+    gat_all,
+    mixed_out,
+    grad_out,
+    total_out,
+    mixed,
+    grad,
+    head,
+    att,
+    gat,
+    tail,
+    in_sem,
+    head_sem,
+    att_sem,
+    out_sem,
+    total_sem,
+):
+    early, parts, local, width = head.shape
+    late = att.shape[0]
+    origins = origins_of(lax.axis_index("col") // 2, early + late)
+
+    def place(j, c):
+        return total_out.at[pl.ds(pl.multiple_of((2 * origins[j] + c) * local, local), local)]
+
+    gat_load = pltpu.make_async_copy(gat_all, gat, in_sem.at[0])
+    gat_load.start()
+    att_loads = {}
+    for j in range(late):
+        for c in range(parts):
+            att_loads[j, c] = pltpu.make_async_copy(att_tail.at[j, c], att.at[j, c], att_sem.at[j, c])
+            att_loads[j, c].start()
+    moves = []
+    for j in range(early):
+        for c in range(parts):
+            moves.append((
+                pltpu.make_async_copy(total_head.at[j, c], head.at[j, c], head_sem.at[j, c]),
+                pltpu.make_async_copy(head.at[j, c], place(j, c), total_sem.at[j, c]),
+            ))
+    moves.append((
+        pltpu.make_async_copy(mixed_in, mixed, in_sem.at[1]),
+        pltpu.make_async_copy(mixed, mixed_out, out_sem.at[0]),
+    ))
+    moves.append((
+        pltpu.make_async_copy(grad_in, grad, in_sem.at[2]),
+        pltpu.make_async_copy(grad, grad_out, out_sem.at[1]),
+    ))
+    for load, store in moves:
+        load.start()
+    gat_load.wait()
+    steps = late * parts
+    share = -(-len(moves) // steps)
+    stores = []
+    for i in range(steps):
+        j, c = divmod(i, parts)
+        att_loads[j, c].wait()
+        tail[j, c] = dot(att[j, c], gat[...], ((0,), (0,))).astype(jnp.bfloat16)
+        stores.append(pltpu.make_async_copy(tail.at[j, c], place(early + j, c), total_sem.at[early + j, c]))
+        stores[-1].start()
+        for load, store in moves[i * share : (i + 1) * share]:
+            load.wait()
+            store.start()
+            stores.append(store)
+    for store in stores:
+        store.wait()
+
+
 def fused_kernel(
     lengths,
+    bucket_ids,
+    sensor_ids,
+    gsd_ids,
+    step_ids,
     qkv,
     weight_hbm,
     cotangent,
-    gate_scene,
+    step_hbm,
+    gsd_table,
+    sensor_table,
+    bucket_table,
     mixed_out,
     grad_out,
-    total_hbm,
+    total_head,
+    att_tail,
+    gat_all,
+    step_table,
     weight,
     att,
     gat,
@@ -149,7 +240,10 @@
     line_recv,
     upstream,
     w_sem,
+    step_sem,
     out_sem,
+    tail_sem,
+    gat_sem,
     att_recv,
     gat_recv,
     pr_recv,
@@ -170,7 +264,8 @@
     half = tok // 2
     nb = weight.shape[0]
     nz = nb // 2
-    scenes = gate_scene.shape[0]
+    scenes = lengths.shape[0]
+    early = total_head.shape[0]
     factor = HEAD ** (-0.5)
     r = lax.axis_index("row")
     col = lax.axis_index("col")
@@ -196,6 +291,8 @@
             weight_hbm.at[pl.ds(b * local, local)], weight.at[b], w_sem.at[b]
         )
 
+    step_load = pltpu.make_async_copy(step_hbm, step_table, step_sem)
+    step_load.start()
     for b in range(nb):
         load(b).start()
 
@@ -213,18 +310,6 @@
         end = end + lengths[s]
         seg_col = seg_col + (place_col >= end).astype(jnp.int32)
         seg_row = seg_row + (place_row >= end).astype(jnp.int32)
-    value = jnp.broadcast_to(gate_scene[0:1, :], (tok, width))
-    for s in range(1, scenes):
-        value = jnp.where(seg_col == s, gate_scene[s : s + 1, :], value)
-    gate[...] = value
-    gat[token_rows(r), :] = (value * cotangent[...].astype(jnp.float32)).astype(jnp.bfloat16)
-
-    def gat_copy(row, part, send, device):
-        rows = gat.at[token_rows(row, part)]
-        return remote(rows, rows, g_sent.at[send], gat_recv.at[row, 0 if part is None else part], device)
-
-    gat_copy(r, None, 0, to_x).start()
-    gat_copy(r, None, 1, to_y).start()
 
     same = seg_col == seg_row
     mine = 2 * z + k
@@ -239,15 +324,7 @@
         out = dot(probs.astype(jnp.bfloat16), qkv[2, :, lanes], ((1,), (0,)))
         att[mine, token_rows(r), lanes] = out.astype(jnp.bfloat16)
 
-    orders = [sorted(range(nz), key=lambda o: (abs(o - p), o)) for p in range(nz)]
-
-    def origin(j):
-        picked = orders[0][j]
-        for p in range(1, nz):
-            picked = jnp.where(z == p, orders[p][j], picked)
-        return picked
-
-    origins = [origin(j) for j in range(nz)]
+    origins = origins_of(z, nz)
 
     def block(row, b, part=None):
         return att.at[b, token_rows(row, part)]
@@ -318,10 +395,17 @@
 
         lax.fori_loop(0, 2, add, 0)
 
-    def out_copy(b):
+    def out_copy(j, c):
         return pltpu.make_async_copy(
-            weight.at[b], total_hbm.at[pl.ds(pl.multiple_of(b * local, local), local)], out_sem.at[b]
+            weight.at[2 * origins[j] + c], total_head.at[j, c], out_sem.at[j, c]
         )
+
+    def tail_copy(j, c):
+        return pltpu.make_async_copy(
+            att.at[2 * origins[j] + c], att_tail.at[j - early, c], tail_sem.at[j - early, c]
+        )
+
+    gat_out = pltpu.make_async_copy(gat, gat_all, gat_sem)
 
     def stage_w(j):
         o = origins[j]
@@ -331,12 +415,42 @@
         def form(c, carry):
             b = 2 * o + c
             weight[b] = dot(att[b], gat[...], ((0,), (0,))).astype(jnp.bfloat16)
-            out_copy(b).start()
+            out_copy(j, c).start()
             return carry
 
-        lax.fori_loop(0, 2, form, 0)
+        if j < early:
+            lax.fori_loop(0, 2, form, 0)
+        else:
+            for c in range(2):
+                tail_copy(j, c).start()
 
     stage_a(0)
+
+    def picks(ids, table):
+        count = table.shape[0]
+        which = lax.broadcasted_iota(jnp.int32, (scenes, count), 0)
+        place = lax.broadcasted_iota(jnp.int32, (scenes, count), 1)
+        wanted = jnp.zeros((scenes, count), jnp.int32)
+        for s in range(scenes):
+            wanted = jnp.where(which == s, ids[s], wanted)
+        chosen = jnp.where(place == wanted, 1.0, 0.0).astype(table.dtype)
+        return dot(chosen, table[...], ((1,), (0,)))
+
+    step_load.wait()
+    gate_scene = picks(step_ids, step_table) + picks(gsd_ids, gsd_table)
+    gate_scene = gate_scene + picks(sensor_ids, sensor_table) + picks(bucket_ids, bucket_table)
+    value = jnp.broadcast_to(gate_scene[0:1, :], (tok, width))
+    for s in range(1, scenes):
+        value = jnp.where(seg_col == s, gate_scene[s : s + 1, :], value)
+    gate[...] = value
+    gat[token_rows(r), :] = (value * cotangent[...].astype(jnp.float32)).astype(jnp.bfloat16)
+
+    def gat_copy(row, part, send, device):
+        rows = gat.at[token_rows(row, part)]
+        return remote(rows, rows, g_sent.at[send], gat_recv.at[row, 0 if part is None else part], device)
+
+    gat_copy(r, None, 0, to_x).start()
+    gat_copy(r, None, 1, to_y).start()
 
     for b in range(nb):
         load(b).wait()
@@ -373,19 +487,23 @@
         line_send[t] = (own[t] + pair_recv[t].astype(jnp.float32)).astype(jnp.bfloat16)
         line_copy(t).start()
 
+    stage_b(0)
     stage_a(1)
+    stage_m(0)
+    stage_c(0)
+    stage_a(2)
     gat_copy(xn, None, 0, to_x).wait_recv()
     gat_copy(xn, 0, 2, to_y).start()
     gat_copy(yn, None, 0, to_x).wait_recv()
     gat_copy(yn, 1, 3, to_x).start()
-    stage_b(0)
-    stage_a(2)
-    stage_m(0)
-    stage_c(0)
     stage_b(1)
     stage_a(3)
     stage_m(1)
     stage_c(1)
+    gat_copy(dn, 0, 0, to_x).wait_recv()
+    gat_copy(dn, 1, 0, to_x).wait_recv()
+    gat_out.start()
+    stage_w(0)
 
     pair_copy(z).wait_recv()
     summed = own[z] + pair_recv[z].astype(jnp.float32)
@@ -417,14 +535,11 @@
     stage_m(2)
     stage_m(3)
     mixed_out[...] = (gate[...] * (total_acc[0] + total_acc[1])).astype(jnp.bfloat16)
-    gat_copy(dn, 0, 0, to_x).wait_recv()
-    gat_copy(dn, 1, 0, to_x).wait_recv()
     stage_c(2)
-    stage_w(0)
+    stage_w(1)
     stage_b(3)
-    stage_w(1)
+    stage_w(2)
     stage_c(3)
-    stage_w(2)
     stage_w(3)
 
     gat_copy(r, None, 0, to_x).wait_send()
@@ -450,10 +565,11 @@
         for row in (r, xn, yn, dn):
             pass_on(row, o).wait_send()
         pair_copy(j).wait_send()
-        out_copy(2 * j).wait()
-        out_copy(2 * j + 1).wait()
+        for c in range(2):
+            (out_copy if j < early else tail_copy)(j, c).wait()
     for d in range(1, nz):
         line_copy(lax.rem(z + d, nz)).wait_send()
+    gat_out.wait()
 
 
 def fused_device(
@@ -475,30 +591,31 @@
     nz = cols // 2
     tok, width = cotangent.shape
     local = qkv.shape[2]
-    gate_scene = lookup(step_ids, step_table) + lookup(gsd_ids, gsd_table)
-    gate_scene = gate_scene + lookup(sensor_ids, sensor_table) + lookup(bucket_ids, bucket_table)
+    early = nz - 1
+    late = nz - early
     dma = pltpu.SemaphoreType.DMA
     bf16 = jnp.bfloat16
-    mixed, grad, total = pl.pallas_call(
+    mixed, grad, head, tail, gat_all = pl.pallas_call(
         fused_kernel,
         out_shape=(
             jax.ShapeDtypeStruct((tok, width), bf16),
             jax.ShapeDtypeStruct((3, tok, local), bf16),
-            jax.ShapeDtypeStruct(out_weight.shape, bf16),
+            jax.ShapeDtypeStruct((early, 2, local, width), bf16),
+            jax.ShapeDtypeStruct((late, 2, rows * tok, local), bf16),
+            jax.ShapeDtypeStruct((rows * tok, width), bf16),
         ),
-        in_specs=[
-            pl.BlockSpec(memory_space=pltpu.SMEM),
+        in_specs=[pl.BlockSpec(memory_space=pltpu.SMEM)] * 5
+        + [
             pl.BlockSpec(memory_space=pltpu.VMEM),
             pl.BlockSpec(memory_space=pl.ANY),
             pl.BlockSpec(memory_space=pltpu.VMEM),
-            pl.BlockSpec(memory_space=pltpu.VMEM),
-        ],
-        out_specs=(
-            pl.BlockSpec(memory_space=pltpu.VMEM),
-            pl.BlockSpec(memory_space=pltpu.VMEM),
             pl.BlockSpec(memory_space=pl.ANY),
-        ),
+        ]
+        + [pl.BlockSpec(memory_space=pltpu.VMEM)] * 3,
+        out_specs=(pl.BlockSpec(memory_space=pltpu.VMEM),) * 2
+        + (pl.BlockSpec(memory_space=pl.ANY),) * 3,
         scratch_shapes=[
+            pltpu.VMEM(step_table.shape, bf16),
             pltpu.VMEM((cols, local, width), bf16),
             pltpu.VMEM((cols, rows * tok, local), bf16),
             pltpu.VMEM((rows * tok, width), bf16),
@@ -512,7 +629,10 @@
             pltpu.VMEM((nz, tok, local), bf16),
             pltpu.VMEM((tok, local), bf16),
             dma((cols,)),
-            dma((cols,)),
+            dma,
+            dma((early, 2)),
+            dma((late, 2)),
+            dma,
             dma((rows, cols, 2)),
             dma((rows, 2)),
             dma((nz,)),
@@ -535,7 +655,49 @@
             bytes_accessed=4 * out_weight.shape[0] * width,
             transcendentals=0,
         ),
-    )(scene_lengths, jnp.transpose(qkv, (1, 0, 2)), out_weight, cotangent, gate_scene)
+    )(
+        scene_lengths,
+        bucket_ids,
+        sensor_ids,
+        gsd_ids,
+        step_ids,
+        jnp.transpose(qkv, (1, 0, 2)),
+        out_weight,
+        cotangent,
+        step_table,
+        gsd_table,
+        sensor_table,
+        bucket_table,
+    )
+    mixed, grad, total = pl.pallas_call(
+        last_kernel,
+        out_shape=(
+            jax.ShapeDtypeStruct(mixed.shape, bf16),
+            jax.ShapeDtypeStruct(grad.shape, bf16),
+            jax.ShapeDtypeStruct(out_weight.shape, bf16),
+        ),
+        in_specs=[pl.BlockSpec(memory_space=pl.ANY)] * 5,
+        out_specs=(pl.BlockSpec(memory_space=pl.ANY),) * 3,
+        scratch_shapes=[
+            pltpu.VMEM(mixed.shape, bf16),
+            pltpu.VMEM(grad.shape, bf16),
+            pltpu.VMEM(head.shape, bf16),
+            pltpu.VMEM(tail.shape, bf16),
+            pltpu.VMEM(gat_all.shape, bf16),
+            pltpu.VMEM((late, 2, local, width), bf16),
+            dma((3,)),
+            dma((early, 2)),
+            dma((late, 2)),
+            dma((2,)),
+            dma((nz, 2)),
+        ],
+        compiler_params=pltpu.CompilerParams(vmem_limit_bytes=60 * 2**20),
+        cost_estimate=pl.CostEstimate(
+            flops=2 * rows * tok * late * 2 * local * width,
+            bytes_accessed=6 * out_weight.shape[0] * width,
+            transcendentals=0,
+        ),
+    )(mixed, grad, head, tail, gat_all)
     return (mixed, jnp.transpose(grad, (1, 0, 2)), total)
 
 

time: 119 us -> 114 us (0.958); the launches traced: 119 us -> 113 us
  local copies, waits for them, and re-layouts: 12.5 us -> 0 us
  Pallas kernels: 103 us -> 112 us
  matrix products: 2.28 us -> 0 us
    unnamed x19 -> x0, local copies, waits for them, and re-layouts: 12.5 us -> none
    pallas_call x0 -> x1, Pallas kernels: none -> 9.61 us  [fused_device(): pl.pallas_call(last_kernel, out_shape=(jax.ShapeDtypeStruct(mixed.shape,...]
    dot_general x4 -> x0, matrix products: 2.28 us -> none  [lookup(): return jnp.dot(picks, table, preferred_element_type=jnp.float32)]
where the time goes in v2:
time: 114 us; the launch traced here: 113 us
  Pallas kernels  112 us (98%)
    pallas_call x1, Pallas kernels, fused_device(): pl.pallas_call(fused_kernel, out_shape=(jax.ShapeDtypeStruct((tok, width)...  102 us
    pallas_call x1, Pallas kernels, fused_device(): pl.pallas_call(last_kernel, out_shape=(jax.ShapeDtypeStruct(mixed.shape,...  9.61 us

profile of v2, /device:TPU:0, one launch (start us, length us, event | category | flops | bytes accessed | tf_op | source)
XLA Modules:
  0.0 112.7 jit_solution(14124354543078313716)
XLA Ops:
  0.6 102.2 %shard_map.139 = (bf16[384,1024]{1,0:T(8,128)(2,1)}, bf16[3,384,512]{2,1,0:T(8,128)(2,1)}, bf16[3,2,512,1024]{3,2,1,0:T(8,128)(2,1)}, bf16[1,2,1536,512]{3,2,1,0:T(8,128)(2,1)}, bf16[1536,1024]{1,0:T(8,128)(2,1)}) custom-call(s32[8]{0:T(128)} %lengths.1, s32[8]{0:T(128)} %bucket_ids.1, s32[8]{0:T(128)} %sensor_ids.1, s32[8]{0:T(128)} %gsd_ids.1, s32[8]{0:T(128)} %step_ids.1, ...), custom_call_target="tpu_custom_call" | custom-call | flops 19327352832 | bytes 16777216 | tf_op jit(solution)/shard_map/pallas_call | solution.py:598
  102.9 9.6 %shard_map.140 = (bf16[384,1024]{1,0:T(8,128)(2,1)}, bf16[3,384,512]{2,1,0:T(8,128)(2,1)}, bf16[4096,1024]{1,0:T(8,128)(2,1)}) custom-call(bf16[384,1024]{1,0:T(8,128)(2,1)} %get-tuple-element.11.mixed_in, bf16[3,384,512]{2,1,0:T(8,128)(2,1)} %get-tuple-element.12.grad_in, bf16[3,2,512,1024]{3,2,1,0:T(8,128)(2,1)} %get-tuple-element.13.total_head, ...), custom_call_target="tpu_custom_call" | custom-call | flops 3221225472 | bytes 25165824 | tf_op jit(solution)/shard_map/pallas_call | solution.py:672

commit v3 on v2

--- a/solution.py
+++ b/solution.py
@@ -339,27 +339,32 @@
     def got(row, b, part=None):
         att_copy(row, b, part, p_sent.at[0, 0], pair).wait_recv()
 
-    def upward(o):
-        return att_copy(r, 2 * o + k, None, z_sent.at[o, 0], {"col": lax.rem(col + 2, 2 * nz)})
-
-    def downward(o):
+    def upward(which, o):
+        row = dn if which else r
         return att_copy(
-            r, 2 * o + k, None, z_sent.at[o, 1], {"col": lax.rem(col + 2 * nz - 2, 2 * nz)}
+            row, 2 * o + k, None, z_sent.at[which, o, 0], {"col": lax.rem(col + 2, 2 * nz)}
         )
+
+    def downward(which, o):
+        row = dn if which else r
+        return att_copy(
+            row, 2 * o + k, None, z_sent.at[which, o, 1], {"col": lax.rem(col + 2 * nz - 2, 2 * nz)}
+        )
+
+    def along_z(which, o):
+        @pl.when((o <= z) & (z < nz - 1))
+        def _():
+            upward(which, o).start()
+
+        @pl.when((o >= z) & (z > 0))
+        def _():
+            downward(which, o).start()
 
     def stage_a(j):
         o = origins[j]
         if j > 0:
             got(r, 2 * o + k)
-
-        @pl.when((o <= z) & (z < nz - 1))
-        def _():
-            upward(o).start()
-
-        @pl.when((o >= z) & (z > 0))
-        def _():
-            downward(o).start()
-
+        along_z(0, o)
         att_copy(r, 2 * o + k, None, x_sent.at[j], to_x).start()
         att_copy(r, 2 * o + k, None, y_sent.at[j], to_y).start()
         pass_on(r, o).start()
@@ -368,16 +373,22 @@
         o = origins[j]
         b = 2 * o + k
         got(xn, b)
-        att_copy(xn, b, 0, fy_sent.at[j], to_y).start()
+        if j == 0:
+            att_copy(xn, b, 0, fy_sent.at[j], to_y).start()
         pass_on(xn, o).start()
         got(yn, b)
-        att_copy(yn, b, 1, fx_sent.at[j], to_x).start()
+        if j == 0:
+            att_copy(yn, b, 1, fx_sent.at[j], to_x).start()
         pass_on(yn, o).start()
 
     def stage_c(j):
         o = origins[j]
-        got(dn, 2 * o + k, 0)
-        got(dn, 2 * o + k, 1)
+        if j == 0:
+            got(dn, 2 * o + k, 0)
+            got(dn, 2 * o + k, 1)
+        else:
+            got(dn, 2 * o + k)
+        along_z(1, o)
         pass_on(dn, o).start()
 
     def stage_m(j):
@@ -476,44 +487,76 @@
 
     lax.fori_loop(0, nz, for_self, 0)
 
-    def line_copy(t):
+    for t in range(nz):
+        pair_copy(t).wait_recv()
+
+    def line_copy(t, down, device):
+        slot = t + nz if down else t
         return remote(
-            line_send.at[t], line_recv.at[z], ls_sent.at[t], lr_recv.at[z], {"col": 2 * t + k}
+            line_send.at[t], line_recv.at[slot], ls_sent.at[t], lr_recv.at[slot], device
         )
 
-    for d in range(1, nz):
-        t = lax.rem(z + d, nz)
-        pair_copy(t).wait_recv()
-        line_send[t] = (own[t] + pair_recv[t].astype(jnp.float32)).astype(jnp.bfloat16)
-        line_copy(t).start()
-
+    def hop(p, t):
+        down = t < p
+        summed = own[t] + pair_recv[t].astype(jnp.float32)
+        if 0 < p < nz - 1:
+            line_copy(t, down, pair).wait_recv()
+            summed = summed + line_recv[t + nz if down else t].astype(jnp.float32)
+        line_send[t] = summed.astype(jnp.bfloat16)
+        to = col - 2 if down else col + 2
+        line_copy(t, down, {"col": lax.rem(to + 2 * nz, 2 * nz)}).start()
+
+    def line_step(tau):
+        for p in range(nz):
+            turns = []
+            for t in range(nz):
+                if t == p:
+                    continue
+                near, far = (p, t) if t > p else (nz - 1 - p, nz - 1 - t)
+                turn = 0 if near == 0 else nz - 1 - far + near
+                if turn == tau:
+                    turns.append((-far, t))
+            if turns:
+
+                @pl.when(z == p)
+                def _():
+                    for _, t in sorted(turns):
+                        hop(p, t)
+
+    line_step(0)
     stage_b(0)
     stage_a(1)
+    line_step(1)
+    stage_c(0)
     stage_m(0)
-    stage_c(0)
     stage_a(2)
+    line_step(2)
     gat_copy(xn, None, 0, to_x).wait_recv()
     gat_copy(xn, 0, 2, to_y).start()
     gat_copy(yn, None, 0, to_x).wait_recv()
     gat_copy(yn, 1, 3, to_x).start()
+    stage_a(3)
     stage_b(1)
-    stage_a(3)
+    stage_c(1)
     stage_m(1)
-    stage_c(1)
     gat_copy(dn, 0, 0, to_x).wait_recv()
     gat_copy(dn, 1, 0, to_x).wait_recv()
     gat_out.start()
     stage_w(0)
 
-    pair_copy(z).wait_recv()
-    summed = own[z] + pair_recv[z].astype(jnp.float32)
-    for d in range(1, nz):
-        t = lax.rem(z + d, nz)
-        remote(
-            line_send.at[t], line_recv.at[t], ls_sent.at[t], lr_recv.at[t], {"col": 2 * t + k}
-        ).wait_recv()
-        summed = summed + line_recv[t].astype(jnp.float32)
-    upstream[...] = summed.astype(jnp.bfloat16)
+    own[z] = own[z] + pair_recv[z].astype(jnp.float32)
+
+    @pl.when(z > 0)
+    def _():
+        line_copy(z, False, pair).wait_recv()
+        own[z] = own[z] + line_recv[z].astype(jnp.float32)
+
+    @pl.when(z < nz - 1)
+    def _():
+        line_copy(z, True, pair).wait_recv()
+        own[z] = own[z] + line_recv[nz + z].astype(jnp.float32)
+
+    upstream[...] = own[z].astype(jnp.bfloat16)
     for h in range(heads):
         lanes = slice(h * HEAD, (h + 1) * HEAD)
         upper = upstream[:, lanes]
@@ -552,23 +595,26 @@
 
         @pl.when((o <= z) & (z < nz - 1))
         def _():
-            upward(o).wait_send()
+            upward(0, o).wait_send()
+            upward(1, o).wait_send()
 
         @pl.when((o >= z) & (z > 0))
         def _():
-            downward(o).wait_send()
+            downward(0, o).wait_send()
+            downward(1, o).wait_send()
 
         att_copy(r, b, None, x_sent.at[j], to_x).wait_send()
         att_copy(r, b, None, y_sent.at[j], to_y).wait_send()
-        att_copy(xn, b, 0, fy_sent.at[j], to_y).wait_send()
-        att_copy(yn, b, 1, fx_sent.at[j], to_x).wait_send()
+        if j == 0:
+            att_copy(xn, b, 0, fy_sent.at[j], to_y).wait_send()
+            att_copy(yn, b, 1, fx_sent.at[j], to_x).wait_send()
         for row in (r, xn, yn, dn):
             pass_on(row, o).wait_send()
         pair_copy(j).wait_send()
         for c in range(2):
             (out_copy if j < early else tail_copy)(j, c).wait()
     for d in range(1, nz):
-        line_copy(lax.rem(z + d, nz)).wait_send()
+        line_copy(lax.rem(z + d, nz), False, pair).wait_send()
     gat_out.wait()
 
 
@@ -626,7 +672,7 @@
             pltpu.VMEM((nz, tok, local), bf16),
             pltpu.VMEM((nz, tok, local), bf16),
             pltpu.VMEM((nz, tok, local), bf16),
-            pltpu.VMEM((nz, tok, local), bf16),
+            pltpu.VMEM((2 * nz, tok, local), bf16),
             pltpu.VMEM((tok, local), bf16),
             dma((cols,)),
             dma,
@@ -636,8 +682,8 @@
             dma((rows, cols, 2)),
             dma((rows, 2)),
             dma((nz,)),
-            dma((nz,)),
-            dma((nz, 2)),
+            dma((2 * nz,)),
+            dma((2, nz, 2)),
             dma((nz,)),
             dma((nz,)),
             dma((nz,)),

time: 114 us -> 108 us (0.947)
  Pallas kernels: 112 us -> 106 us
    pallas_call x1, Pallas kernels: 102 us -> 96.1 us  [fused_device(): pl.pallas_call(fused_kernel, out_shape=(jax.ShapeDtypeStruct((tok, width)...]
where the time goes in v3:
time: 108 us; the launch traced here: 107 us
  Pallas kernels  106 us (98%)
    pallas_call x1, Pallas kernels, fused_device(): pl.pallas_call(fused_kernel, out_shape=(jax.ShapeDtypeStruct((tok, width)...  96.1 us
    pallas_call x1, Pallas kernels, fused_device(): pl.pallas_call(last_kernel, out_shape=(jax.ShapeDtypeStruct(mixed.shape,...  9.61 us

profile of v3, /device:TPU:0, one launch (start us, length us, event | category | flops | bytes accessed | tf_op | source)
XLA Modules:
  0.0 106.6 jit_solution(12513184014229070233)
XLA Ops:
  0.6 96.1 %shard_map.139 = (bf16[384,1024]{1,0:T(8,128)(2,1)}, bf16[3,384,512]{2,1,0:T(8,128)(2,1)}, bf16[3,2,512,1024]{3,2,1,0:T(8,128)(2,1)}, bf16[1,2,1536,512]{3,2,1,0:T(8,128)(2,1)}, bf16[1536,1024]{1,0:T(8,128)(2,1)}) custom-call(s32[8]{0:T(128)} %lengths.1, s32[8]{0:T(128)} %bucket_ids.1, s32[8]{0:T(128)} %sensor_ids.1, s32[8]{0:T(128)} %gsd_ids.1, s32[8]{0:T(128)} %step_ids.1, ...), custom_call_target="tpu_custom_call" | custom-call | flops 19327352832 | bytes 16777216 | tf_op jit(solution)/shard_map/pallas_call | solution.py:644
  96.8 9.6 %shard_map.140 = (bf16[384,1024]{1,0:T(8,128)(2,1)}, bf16[3,384,512]{2,1,0:T(8,128)(2,1)}, bf16[4096,1024]{1,0:T(8,128)(2,1)}) custom-call(bf16[384,1024]{1,0:T(8,128)(2,1)} %get-tuple-element.11.mixed_in, bf16[3,384,512]{2,1,0:T(8,128)(2,1)} %get-tuple-element.12.grad_in, bf16[3,2,512,1024]{3,2,1,0:T(8,128)(2,1)} %get-tuple-element.13.total_head, ...), custom_call_target="tpu_custom_call" | custom-call | flops 3221225472 | bytes 25165824 | tf_op jit(solution)/shard_map/pallas_call | solution.py:718

commit v4 on v3

--- a/solution.py
+++ b/solution.py
@@ -128,7 +128,9 @@
 
 
 def origins_of(z, nz):
-    orders = [sorted(range(nz), key=lambda o: (abs(o - p), o)) for p in range(nz)]
+    orders = [
+        sorted(range(nz), key=lambda o: (abs(o - p), -o if 2 * p < nz else o)) for p in range(nz)
+    ]
     origins = []
     for j in range(nz):
         picked = orders[0][j]
@@ -365,9 +367,12 @@
         if j > 0:
             got(r, 2 * o + k)
         along_z(0, o)
+        pass_on(r, o).start()
+
+    def over_plane(j):
+        o = origins[j]
         att_copy(r, 2 * o + k, None, x_sent.at[j], to_x).start()
         att_copy(r, 2 * o + k, None, y_sent.at[j], to_y).start()
-        pass_on(r, o).start()
 
     def stage_b(j):
         o = origins[j]
@@ -435,6 +440,7 @@
             for c in range(2):
                 tail_copy(j, c).start()
 
+    over_plane(0)
     stage_a(0)
 
     def picks(ids, table):
@@ -460,8 +466,6 @@
         rows = gat.at[token_rows(row, part)]
         return remote(rows, rows, g_sent.at[send], gat_recv.at[row, 0 if part is None else part], device)
 
-    gat_copy(r, None, 0, to_x).start()
-    gat_copy(r, None, 1, to_y).start()
 
     for b in range(nb):
         load(b).wait()
@@ -479,6 +483,11 @@
         return carry
 
     lax.fori_loop(0, nz, for_pair, 0)
+    stage_b(0)
+    gat_copy(r, None, 0, to_x).start()
+    gat_copy(r, None, 1, to_y).start()
+    stage_a(1)
+    over_plane(1)
 
     def for_self(i, carry):
         t = lax.rem(z + 1 + i, nz)
@@ -523,26 +532,32 @@
                     for _, t in sorted(turns):
                         hop(p, t)
 
+    stage_a(2)
+    stage_c(0)
     line_step(0)
-    stage_b(0)
-    stage_a(1)
-    line_step(1)
-    stage_c(0)
     stage_m(0)
-    stage_a(2)
-    line_step(2)
+    stage_a(3)
+    stage_c(1)
     gat_copy(xn, None, 0, to_x).wait_recv()
     gat_copy(xn, 0, 2, to_y).start()
     gat_copy(yn, None, 0, to_x).wait_recv()
     gat_copy(yn, 1, 3, to_x).start()
-    stage_a(3)
+    over_plane(2)
+    over_plane(3)
+    line_step(1)
+    stage_m(1)
+    line_step(2)
     stage_b(1)
-    stage_c(1)
-    stage_m(1)
-    gat_copy(dn, 0, 0, to_x).wait_recv()
-    gat_copy(dn, 1, 0, to_x).wait_recv()
-    gat_out.start()
-    stage_w(0)
+    stage_c(2)
+    stage_m(2)
+    stage_m(3)
+    mixed_out[...] = (gate[...] * (total_acc[0] + total_acc[1])).astype(jnp.bfloat16)
+
+    inner_chip = (z > 0) & (z < nz - 1)
+
+    @pl.when(inner_chip)
+    def _():
+        stage_c(3)
 
     own[z] = own[z] + pair_recv[z].astype(jnp.float32)
 
@@ -574,15 +589,19 @@
             dot(grad_scores, qkv[0, :, lanes], ((0,), (0,))) * factor
         ).astype(jnp.bfloat16)
 
+    gat_copy(dn, 0, 0, to_x).wait_recv()
+    gat_copy(dn, 1, 0, to_x).wait_recv()
+    gat_out.start()
+    stage_w(0)
     stage_b(2)
-    stage_m(2)
-    stage_m(3)
-    mixed_out[...] = (gate[...] * (total_acc[0] + total_acc[1])).astype(jnp.bfloat16)
-    stage_c(2)
     stage_w(1)
+
+    @pl.when(jnp.logical_not(inner_chip))
+    def _():
+        stage_c(3)
+
     stage_b(3)
     stage_w(2)
-    stage_c(3)
     stage_w(3)
 
     gat_copy(r, None, 0, to_x).wait_send()

time: 108 us -> 98.7 us (0.914)
  Pallas kernels: 106 us -> 96.6 us
    pallas_call x1, Pallas kernels: 96.1 us -> 87 us  [fused_device(): pl.pallas_call(fused_kernel, out_shape=(jax.ShapeDtypeStruct((tok, width)...]
where the time goes in v4:
time: 98.7 us; the launch traced here: 97.4 us
  Pallas kernels  96.6 us (98%)
    pallas_call x1, Pallas kernels, fused_device(): pl.pallas_call(fused_kernel, out_shape=(jax.ShapeDtypeStruct((tok, width)...  87 us
    pallas_call x1, Pallas kernels, fused_device(): pl.pallas_call(last_kernel, out_shape=(jax.ShapeDtypeStruct(mixed.shape,...  9.6 us

profile of v4, /device:TPU:0, one launch (start us, length us, event | category | flops | bytes accessed | tf_op | source)
XLA Modules:
  0.0 97.4 jit_solution(4724005549683292805)
XLA Ops:
  0.6 87.0 %shard_map.139 = (bf16[384,1024]{1,0:T(8,128)(2,1)}, bf16[3,384,512]{2,1,0:T(8,128)(2,1)}, bf16[3,2,512,1024]{3,2,1,0:T(8,128)(2,1)}, bf16[1,2,1536,512]{3,2,1,0:T(8,128)(2,1)}, bf16[1536,1024]{1,0:T(8,128)(2,1)}) custom-call(s32[8]{0:T(128)} %lengths.1, s32[8]{0:T(128)} %bucket_ids.1, s32[8]{0:T(128)} %sensor_ids.1, s32[8]{0:T(128)} %gsd_ids.1, s32[8]{0:T(128)} %step_ids.1, ...), custom_call_target="tpu_custom_call" | custom-call | flops 19327352832 | bytes 16777216 | tf_op jit(solution)/shard_map/pallas_call | solution.py:663
  87.7 9.6 %shard_map.140 = (bf16[384,1024]{1,0:T(8,128)(2,1)}, bf16[3,384,512]{2,1,0:T(8,128)(2,1)}, bf16[4096,1024]{1,0:T(8,128)(2,1)}) custom-call(bf16[384,1024]{1,0:T(8,128)(2,1)} %get-tuple-element.11.mixed_in, bf16[3,384,512]{2,1,0:T(8,128)(2,1)} %get-tuple-element.12.grad_in, bf16[3,2,512,1024]{3,2,1,0:T(8,128)(2,1)} %get-tuple-element.13.total_head, ...), custom_call_target="tpu_custom_call" | custom-call | flops 3221225472 | bytes 25165824 | tf_op jit(solution)/shard_map/pallas_call | solution.py:737

commit v5 on v4

--- a/solution.py
+++ b/solution.py
@@ -656,7 +656,7 @@
     nz = cols // 2
     tok, width = cotangent.shape
     local = qkv.shape[2]
-    early = nz - 1
+    early = nz - 2
     late = nz - early
     dma = pltpu.SemaphoreType.DMA
     bf16 = jnp.bfloat16

time: 98.7 us -> 98.6 us (level)
  the two profiles are of different devices: /device:TPU:0 before, /device:TPU:9 now
where the time goes in v5:
time: 98.6 us; the launch traced here: 98.5 us
  Pallas kernels  97.6 us (99%)
    pallas_call x1, Pallas kernels, fused_device(): pl.pallas_call(fused_kernel, out_shape=(jax.ShapeDtypeStruct((tok, width)...  86.5 us
    pallas_call x1, Pallas kernels, fused_device(): pl.pallas_call(last_kernel, out_shape=(jax.ShapeDtypeStruct(mixed.shape,...  11.1 us

profile of v5, /device:TPU:9, one launch (start us, length us, event | category | flops | bytes accessed | tf_op | source)
XLA Modules:
  0.0 98.5 jit_solution(7479411421089233659)
XLA Ops:
  0.6 86.5 %shard_map.139 = (bf16[384,1024]{1,0:T(8,128)(2,1)}, bf16[3,384,512]{2,1,0:T(8,128)(2,1)}, bf16[2,2,512,1024]{3,2,1,0:T(8,128)(2,1)}, bf16[2,2,1536,512]{3,2,1,0:T(8,128)(2,1)}, bf16[1536,1024]{1,0:T(8,128)(2,1)}) custom-call(s32[8]{0:T(128)} %lengths.1, s32[8]{0:T(128)} %bucket_ids.1, s32[8]{0:T(128)} %sensor_ids.1, s32[8]{0:T(128)} %gsd_ids.1, s32[8]{0:T(128)} %step_ids.1, ...), custom_call_target="tpu_custom_call" | custom-call | flops 19327352832 | bytes 16777216 | tf_op jit(solution)/shard_map/pallas_call | solution.py:663
  87.2 11.1 %shard_map.140 = (bf16[384,1024]{1,0:T(8,128)(2,1)}, bf16[3,384,512]{2,1,0:T(8,128)(2,1)}, bf16[4096,1024]{1,0:T(8,128)(2,1)}) custom-call(bf16[384,1024]{1,0:T(8,128)(2,1)} %get-tuple-element.11.mixed_in, bf16[3,384,512]{2,1,0:T(8,128)(2,1)} %get-tuple-element.12.grad_in, bf16[2,2,512,1024]{3,2,1,0:T(8,128)(2,1)} %get-tuple-element.13.total_head, ...), custom_call_target="tpu_custom_call" | custom-call | flops 6442450944 | bytes 25165824 | tf_op jit(solution)/shard_map/pallas_call | solution.py:737
